TPU v7x, 256 devices: a whole 4x4x8 slice. The times are simulated.
256 devices in a mesh: dp: 4 (over y), row: 8 (over z), col: 8 (over x, core).
Axes of the slice: x: 4, y: 4, z: 8, core: 2. Of those that a mesh axis runs over, the one named last changes fastest.
Arguments:
- activations: bfloat16 [1024, 16384], P(('dp', 'col'), 'row'), may hold values from -6 to 6
- w_gate: bfloat16 [16384, 28672], P('row', ('dp', 'col')), may hold values from -0.046875 to 0.046875
- w_up: bfloat16 [16384, 28672], P('row', ('dp', 'col')), may hold values from -0.046875 to 0.046875
- w_down: bfloat16 [28672, 16384], P(('dp', 'col'), 'row'), may hold values from -0.03125 to 0.03125
- seq_lengths: int32 [4, 2], P('dp'), may hold values from 1 to 128
Outputs:
- block_out: bfloat16 [1024, 16384], P(('dp', 'col'), 'row')
All inputs are finite; a program needn't handle non-finite values.
Results may differ from a plain program's by a relative error of at most 0.0049.
Values may be sent and summed in bfloat16 or wider, within the bound.
A program may use at most 128 MiB of HBM per device.

v0:
```python
import jax
import jax.numpy as jnp
from jax import lax
from jax.sharding import PartitionSpec as P


def gated(sums, width):
    return (jax.nn.silu(sums[:, :width]) * sums[:, width:]).astype(jnp.bfloat16)


def local(activations, w_gate, w_up, w_down, seq_lengths):
    width = w_gate.shape[1]
    panel = lax.all_gather(activations, ("dp", "col"), axis=0, tiled=True)
    gate_part = jnp.dot(panel, w_gate, preferred_element_type=jnp.float32)
    up_part = jnp.dot(panel, w_up, preferred_element_type=jnp.float32)
    partial_value = jnp.concatenate([gate_part, up_part], axis=1)
    summed = lax.psum(partial_value, "row")
    hidden = gated(summed, width)
    own_rows = activations.shape[0]
    projected = lax.psum_scatter(
        jnp.dot(hidden, w_down, preferred_element_type=jnp.float32),
        ("dp", "col"),
        scatter_dimension=0,
        tiled=True,
    )
    group_size = own_rows * lax.axis_size("col")
    seq_count = seq_lengths.shape[1]
    slot_len = group_size // seq_count
    within = lax.axis_index("col") * own_rows + jnp.arange(own_rows, dtype=jnp.int32)
    seq_index = within // slot_len
    offset = within % slot_len
    selected = seq_index[:, None] == jnp.arange(seq_count, dtype=jnp.int32)[None, :]
    limits = jnp.sum(jnp.where(selected, seq_lengths[0][None, :], 0), axis=1)
    keep = (offset < limits).astype(jnp.float32)
    return (projected * keep[:, None]).astype(jnp.bfloat16)


def solution(mesh):
    return jax.shard_map(
        local,
        mesh=mesh,
        in_specs=(
            P(("dp", "col"), "row"),
            P("row", ("dp", "col")),
            P("row", ("dp", "col")),
            P(("dp", "col"), "row"),
            P("dp", None),
        ),
        out_specs=P(("dp", "col"), "row"),
        check_vma=False,
    )
```

profile of v0, /device:TPU:9, one launch (start us, length us, event | category | flops | bytes accessed | tf_op | source)
XLA Modules:
  0.0 364.5 jit_solution(14154848026414570496)
XLA Ops:
  6.5 0.0 all-gather.2.cloned.1.call-start
  6.5 0.7 all-gather.2.cloned.1.call-update
  7.3 0.0 all-reduce.2.cloned.1.call-start
  7.3 56.7 %all-gather.2.cloned.1.call-done = bf16[1024,2048]{1,0:T(8,128)(2,1)} async-done(((bf16[32,2048]{1,0:T(8,128)(2,1)}), bf16[1024,2048]{1,0:T(8,128)(2,1)}) %all-gather.2.cloned.1.call-update) | async-done | bytes 4194320 | tf_op jit(solution)/shard_map/all_gather | solution.py:13
  64.0 0.0 copy-start
  64.0 0.0 copy-start.1
  64.0 7.1 %fusion.6 = f32[1024,896]{0,1:T(8,128)S(1)} fusion(bf16[1024,2048]{1,0:T(8,128)(2,1)} %all-gather.2.cloned.1.call-done, bf16[2048,896]{1,0:T(8,128)(2,1)} %param.6), kind=kOutput, calls=%fused_computation.16 | convolution fusion | flops 3758096384 | bytes 11534336 | tf_op jit(solution)/shard_map/dot_general | solution.py:14
  71.1 0.0 copy-done
  71.1 0.0 copy-done.1
  71.1 4.2 %fusion.7 = f32[1024,896]{0,1:T(8,128)S(1)} fusion(bf16[1024,2048]{1,0:T(8,128)(2,1)S(1)} %copy-done, bf16[2048,896]{1,0:T(8,128)(2,1)S(1)} %copy-done.1), kind=kOutput, calls=%fused_computation.17 | convolution fusion | flops 3758096384 | bytes 11534336 | tf_op jit(solution)/shard_map/dot_general | solution.py:15
  75.3 3.7 %pad_maximum_fusion = f32[1024,1792]{0,1:T(8,128)} fusion(f32[1024,896]{0,1:T(8,128)S(1)} %fusion.7, f32[1024,896]{0,1:T(8,128)S(1)} %fusion.6), kind=kLoop, calls=%fused_computation | loop fusion | flops 1835008 | bytes 14680064 | tf_op jit(solution)/shard_map/concatenate | solution.py:16
  79.0 0.0 all-reduce.2.cloned.1.call-update
  79.0 0.0 reduce-scatter.2.cloned.1.call-start
  79.1 167.7 %all-reduce.2.cloned.1.call-done = f32[1024,1792]{0,1:T(8,128)} async-done(((f32[1024,1792]{0,1:T(8,128)}), f32[1024,1792]{0,1:T(8,128)}) %all-reduce.2.cloned.1.call-update) | async-done | bytes 7340048 | tf_op jit(solution)/shard_map/psum | solution.py:17
  246.8 12.0 %fusion.1 = f32[1024,2048]{1,0:T(8,128)} fusion(bf16[896,2048]{1,0:T(8,128)(2,1)} %param.8, f32[1024,1792]{0,1:T(8,128)} %all-reduce.2.cloned.1.call-done), kind=kOutput, calls=%fused_computation.3 | convolution fusion | flops 3763601408 | bytes 19398656 | tf_op jit(solution)/shard_map/dot_general | solution.py:21
  258.8 0.0 copy-start.2
  258.8 0.0 reduce-scatter.2.cloned.1.call-update
  258.9 0.6 copy-done.2
  259.5 0.1 fusion.4
  259.6 96.7 %reduce-scatter.2.cloned.1.call-done = f32[32,2048]{1,0:T(8,128)} async-done(((f32[1024,2048]{1,0:T(8,128)}), f32[32,2048]{1,0:T(8,128)}) %reduce-scatter.2.cloned.1.call-update) | async-done | bytes 262160 | tf_op jit(solution)/shard_map/reduce_scatter | solution.py:20
  356.2 1.7 multiply_convert_fusion
  (2 shorter events, 0.0 us)
Async XLA Ops:
  6.5 57.5 %all-gather.2.cloned.1.call-start = ((), (), s32[]{:S(2)}) async-start(), calls=%async_computation.1 | async-start | bytes 4325376 | tf_op jit(solution)/shard_map/all_gather | solution.py:13
  7.3 239.5 %all-reduce.2.cloned.1.call-start = ((), (), s32[]{:S(2)}) async-start(), calls=%async_computation.2 | async-start | bytes 14680064 | tf_op jit(solution)/shard_map/psum | solution.py:17
  64.0 7.1 %copy-start = (bf16[1024,2048]{1,0:T(8,128)(2,1)S(1)}, bf16[1024,2048]{1,0:T(8,128)(2,1)}, u32[]{:S(2)}) copy-start(bf16[1024,2048]{1,0:T(8,128)(2,1)} %all-gather.2.cloned.1.call-done) | copy-start | bytes 12582916
  64.0 7.1 %copy-start.1 = (bf16[2048,896]{1,0:T(8,128)(2,1)S(1)}, bf16[2048,896]{1,0:T(8,128)(2,1)}, u32[]{:S(2)}) copy-start(bf16[2048,896]{1,0:T(8,128)(2,1)} %param.7) | copy-start | bytes 11010052
  79.0 277.2 %reduce-scatter.2.cloned.1.call-start = ((), (), s32[]{:S(2)}) async-start(), calls=%async_computation.3 | async-start | bytes 8650752 | tf_op jit(solution)/shard_map/reduce_scatter | solution.py:20
  258.8 0.7 copy-start.2
Sparse Core Ops, SparseCore 0:
  9.9 54.0 all-gather.1
  79.1 167.5 all-reduce.1
  259.0 97.2 reduce-scatter.1
where the time goes:
time: 366 us; the launch traced here: 364 us
  waiting for transfers between devices  322 us (88%)
  matrix products  23.3 us (6%)
  between operations  13.2 us (4%)
  other arithmetic  5.46 us (1%)
    psum x1, waiting for transfers between devices, local(): summed = lax.psum(partial_value, 'row')  168 us
    reduce_scatter x1, waiting for transfers between devices, local(): lax.psum_scatter(jnp.dot(hidden, w_down, preferred_element_type=jnp.float...  96.7 us
    all_gather x1, waiting for transfers between devices, local(): panel = lax.all_gather(activations, ('dp', 'col'), axis=0, tiled=True)  56.7 us
    dot_general x1, matrix products, local(): jnp.dot(hidden, w_down, preferred_element_type=jnp.float32)  12 us
  transfers between devices with their start and end apart: 3, of which 3 were waited for; matrix products, arithmetic and copies ran while one was open for 0% of the time, Pallas kernels for 0%

commit v1 on v0

v1 whole, which is shorter than its diff:
```python
import jax
import jax.numpy as jnp
from jax import lax
from jax.experimental import pallas as pl
from jax.experimental.pallas import tpu as pltpu
from jax.sharding import PartitionSpec as P

MESH = pl.DeviceIdType.MESH
BF, F32 = jnp.bfloat16, jnp.float32
ROWS = 16
UNIT = 128
UNITS = [(0, 0), (1, 0), (3, 0), (2, 0), (1, 1), (2, 1), (3, 1), (0, 1)]
SUMS = ['two', 'chain', 'chain', 'chainf', 'chain', 'chain', 'chain', 'chain']
GATHERS = ['chain', 'chain', 'chain', 'chain', 'chain', 'chain', 'chain', 'chain']
ORDER = [
    ("x", 0), ("x", 1), ("bx", 0, 1), ("bx", 0, 3), ("bx", 0, 2), ("bx", 1, 1), ("bx", 1, 3), ("mm", 0, 0),
    ("mm", 0, 1), ("bx", 1, 2), ("mm", 7, 0), ("by", 1, 0), ("by", 3, 0), ("mm", 7, 1), ("mm", 1, 0),
    ("mm", 1, 1), ("r", 0, 1, 1), ("r", 0, 1, 0), ("mm", 2, 0), ("mm", 2, 1), ("r", 1, 1, 0), ("r", 1, 1, 1),
    ("by", 1, 1), ("by", 3, 1), ("r", 7, 1, 0), ("r", 7, 1, 1), ("mm", 4, 0), ("r", 2, 1, 1), ("g", 0),
    ("r", 2, 1, 0), ("by", 2, 0), ("r", 1, 2, 1), ("r", 1, 2, 0), ("mm", 4, 1), ("mm", 3, 0), ("r", 2, 2, 1),
    ("a", 0, 1, 0), ("a", 0, 1, 1), ("r", 4, 1, 0), ("mm", 3, 1), ("r", 1, 3, 1), ("r", 2, 2, 0), ("r", 1, 3, 0),
    ("r", 4, 1, 1), ("r", 3, 1, 0), ("by", 2, 1), ("r", 2, 3, 1), ("a", 0, 2, 0), ("a", 0, 2, 1), ("mm", 6, 0),
    ("mm", 5, 0), ("r", 2, 3, 0), ("r", 3, 1, 1), ("r", 4, 2, 0), ("mm", 5, 1), ("r", 4, 2, 1), ("g", 1),
    ("mm", 6, 1), ("a", 0, 3, 0), ("r", 6, 1, 0), ("a", 0, 3, 1), ("r", 3, 2, 1), ("r", 5, 1, 0), ("r", 3, 2, 0),
    ("r", 7, 2, 1), ("g", 2), ("r", 4, 3, 1), ("r", 5, 1, 1), ("a", 1, 1, 1), ("r", 4, 3, 0), ("r", 6, 1, 1),
    ("a", 1, 1, 0), ("pj", 0), ("r", 3, 3, 1), ("r", 6, 2, 0), ("r", 7, 2, 0), ("r", 7, 3, 1), ("r", 5, 2, 0),
    ("a", 2, 1, 1), ("sc", 0), ("r", 3, 3, 0), ("a", 2, 1, 0), ("r", 5, 2, 1), ("g", 4), ("a", 1, 2, 1),
    ("a", 1, 2, 0), ("r", 6, 2, 1), ("r", 6, 3, 0), ("r", 7, 3, 0), ("ty", 0), ("r", 5, 3, 0), ("a", 2, 2, 1),
    ("g", 3), ("r", 5, 3, 1), ("a", 2, 2, 0), ("a", 4, 1, 1), ("a", 4, 1, 0), ("a", 1, 3, 1), ("a", 1, 3, 0),
    ("r", 6, 3, 1), ("a", 2, 3, 1), ("a", 3, 1, 1), ("g", 7), ("g", 5), ("a", 4, 2, 1), ("a", 3, 1, 0),
    ("a", 2, 3, 0), ("a", 4, 2, 0), ("g", 6), ("pj", 1), ("a", 5, 1, 0), ("a", 7, 1, 1), ("a", 3, 2, 1),
    ("a", 3, 2, 0), ("a", 5, 1, 1), ("pj", 2), ("a", 4, 3, 0), ("sc", 1), ("a", 4, 3, 1), ("a", 5, 2, 0),
    ("a", 7, 2, 1), ("a", 6, 1, 1), ("a", 6, 1, 0), ("a", 3, 3, 0), ("a", 3, 3, 1), ("sc", 2), ("a", 5, 2, 1),
    ("a", 7, 1, 0), ("pj", 4), ("a", 7, 3, 1), ("a", 5, 3, 0), ("a", 6, 2, 1), ("a", 6, 2, 0), ("pj", 3),
    ("a", 5, 3, 1), ("a", 7, 2, 0), ("sc", 4), ("ty", 1), ("a", 6, 3, 1), ("a", 6, 3, 0), ("sc", 3), ("pj", 5),
    ("a", 7, 3, 0), ("ty", 2), ("pj", 6), ("sc", 5), ("pj", 7), ("ty", 4), ("sc", 6), ("ty", 3), ("sc", 7),
    ("ty", 5), ("ty", 6), ("ty", 7),
]
SLOT = {unit: i for i, unit in enumerate(UNITS)}
N = len(UNITS)
WIDE = [u for u in range(N) if SUMS[u] == "chainf"]
N_WIDE = max(1, len(WIDE))


def kernel(act, w_gate, w_up, w_down, lens, out, panel, wgu, wdn, part, rs_out, rs_in, wide_out, wide_in, hid, proj,
           swap_in, x_out, x_in, y_out, y_in, acc, w_sem, ax_s, ax_r, ak_s, ak_r, ay_s, ay_r, rs_s, rs_r, ag_s, ag_r,
           k_s, k_r, x_s, x_r, y_s, y_r):
    y, z, c = lax.axis_index("dp"), lax.axis_index("row"), lax.axis_index("col")
    x, k = c // 2, lax.rem(c, 2)
    ff = w_gate.shape[1]
    width = w_down.shape[1]
    half_cut = 512

    def at_x(step):
        return (y, z, 2 * lax.rem(x + step, 4) + k)

    def at_y(step):
        return (lax.rem(y + step, 4), z, c)

    def at_z(step):
        return (y, lax.rem(z + step + 8, 8), c)

    sibling = (y, z, 2 * x + 1 - k)
    peers = [at_x(1), at_x(2), at_x(3), at_y(1), at_y(2), at_y(3), at_z(1), at_z(-1), at_z(2), at_z(-2), sibling]
    sent, live = [], {}

    def send(name, src, dst, ss, rs, device):
        copy = pltpu.make_async_remote_copy(src_ref=src, dst_ref=dst, send_sem=ss, recv_sem=rs, device_id=device,
                                            device_id_type=MESH)
        copy.start()
        sent.append(copy)
        live[name] = copy

    def arrived(*name):
        live.pop(name).wait_recv()

    weights = [
        pltpu.make_async_copy(w_gate, wgu.at[:, 0:ff], w_sem.at[0]),
        pltpu.make_async_copy(w_up, wgu.at[:, ff:2 * ff], w_sem.at[1]),
        pltpu.make_async_copy(w_down, wdn, w_sem.at[2]),
    ]
    barrier = pltpu.get_barrier_semaphore()
    for peer in peers:
        pl.semaphore_signal(barrier, inc=1, device_id=peer, device_id_type=MESH)
    for copy in weights:
        copy.start()
    pl.semaphore_wait(barrier, len(peers))
    loaded = set()

    def load(i):
        if i not in loaded:
            loaded.add(i)
            weights[i].wait()

    def block(plane, place):
        return pl.ds(pl.multiple_of((plane * 4 + place) * ROWS, ROWS), ROWS)

    def plane(which):
        return pl.ds(pl.multiple_of(which * 4 * ROWS, 4 * ROWS), 4 * ROWS)

    def chunk(step):
        return pl.ds(pl.multiple_of(lax.rem(z + step + 8, 8) * ROWS, ROWS), ROWS)

    def to_column(half, i, src):
        place = lax.rem(x + 4 - i, 4)
        slot = SLOT[(0, half)]
        send(("sb", slot, i), src, panel.at[slot, block(k, place)], ak_s.at[slot, i], ak_r.at[slot, i], sibling)
        for step in (1, 3):
            there = SLOT[(4 - step, half)]
            send(("ay", there, i), src, panel.at[there, block(k, place)], ay_s.at[there, i], ay_r.at[there, i],
                 at_y(step))

    def op_x(half):
        rows = pl.ds(half * ROWS, ROWS)
        slot = SLOT[(0, half)]
        for step in (1, 3, 2):
            send(("ax", half, step), act.at[rows], panel.at[slot, block(k, x)], ax_s.at[half, step - 1],
                 ax_r.at[half, step - 1], at_x(step))
        to_column(half, 0, act.at[rows])
        panel[slot, block(k, x), :] = act[rows, :]

    def op_bx(half, i):
        arrived("ax", half, i)
        to_column(half, i, panel.at[SLOT[(0, half)], block(k, lax.rem(x + 4 - i, 4))])

    def op_by(shift, half):
        slot = SLOT[(shift, half)]
        for i in range(1 if shift == 2 else 4):
            arrived("ay", slot, i)
        mine = panel.at[slot, plane(k)]
        send(("sb", slot, 0), mine, mine, ak_s.at[slot, 0], ak_r.at[slot, 0], sibling)
        if (shift, half) in ((1, 0), (3, 1)):
            there = SLOT[(2, half)]
            send(("ay", there, 0), mine, panel.at[there, plane(k)], ay_s.at[there, 0], ay_r.at[there, 0],
                 at_y(4 - shift))

    every, first, second = slice(0, 2 * ff), slice(0, ff), slice(ff, 2 * ff)
    sign = (1, -1)

    def send_sum(u, way, s, cols, hops):
        send(("r", u, s, way), rs_out.at[u, way, s, :, cols], rs_in.at[u, way, s, :, cols], rs_s.at[u, way, s],
             rs_r.at[u, way, s], at_z(sign[way] * hops))

    def op_mm(u, part_no):
        shift, half = UNITS[u]
        cols = (first, second)[part_no]
        if part_no == 0:
            for i in range(1 if shift else 4):
                arrived("sb", u, i)
        load(part_no)
        part[u, :, cols] = jnp.dot(panel[u], wgu[:, cols], preferred_element_type=F32)
        far = 2 if SUMS[u] == "two" else 1
        rs_out[u, part_no, 0, :, cols] = part[u, chunk(4), cols].astype(BF)
        send_sum(u, part_no, 0, cols, far)
        if SUMS[u] == "two" and part_no == 1:
            for s, dist in ((1, 3), (3, 1)):
                for way in range(2):
                    rs_out[u, way, s] = part[u, chunk(sign[way] * dist), :].astype(BF)
                    send_sum(u, way, s, every, 1)

    def op_r(u, s, way):
        rows = chunk(sign[way] * (2 if SUMS[u] == "two" else 4 - s))
        got, rest = (first, second) if way == 0 else (second, first)
        arrived("r", u, s - 1, way)
        if SUMS[u] == "two":
            arrived("r", u, 1, way)
            rs_out[u, way, 2, :, got] = (part[u, rows, got] + rs_in[u, way, 1, :, got].astype(F32)
                                         + rs_in[u, way, 0, :, got].astype(F32)).astype(BF)
            rs_out[u, way, 2, :, rest] = (part[u, rows, rest] + rs_in[u, way, 1, :, rest].astype(F32)).astype(BF)
            send_sum(u, way, 2, every, 2)
        elif s == 3 and u in WIDE:
            i = WIDE.index(u)
            wide_out[i, way] = part[u, rows, :] + rs_in[u, way, 2].astype(F32)
            send(("r", u, s, way), wide_out.at[i, way], wide_in.at[i, way], rs_s.at[u, way, s], rs_r.at[u, way, s],
                 at_z(sign[way]))
        else:
            if s == 1:
                rs_out[u, way, s, :, got] = (part[u, rows, got] + rs_in[u, way, 0, :, got].astype(F32)).astype(BF)
                rs_out[u, way, s, :, rest] = part[u, rows, rest].astype(BF)
            else:
                rs_out[u, way, s] = (part[u, rows, :] + rs_in[u, way, s - 1].astype(F32)).astype(BF)
            send_sum(u, way, s, every, 1)

    def send_hidden(u, s, way, hops):
        behind = s if GATHERS[u] == "chain" else {0: 0, 1: 0, 2: 2, 3: 2}[s]
        piece = hid.at[u, chunk(-sign[way] * behind)]
        if s == 3:
            cols = slice(0, half_cut) if way == 0 else slice(half_cut, ff)
            piece = hid.at[u, chunk(-sign[way] * behind), cols]
        send(("a", u, s, way), piece, piece, ag_s.at[u, way, s], ag_r.at[u, way, s], at_z(sign[way] * hops))

    def op_g(u):
        rows = chunk(0)
        total = part[u, rows, :]
        for way in range(2):
            arrived("r", u, 3, way)
            if u in WIDE:
                total += wide_in[WIDE.index(u), way]
            else:
                total += rs_in[u, way, 3].astype(F32)
            if SUMS[u] == "two":
                arrived("r", u, 2, way)
                total += rs_in[u, way, 2].astype(F32)
        hid[u, rows, :] = (jax.nn.silu(total[:, :ff]) * total[:, ff:]).astype(BF)
        if GATHERS[u] == "two":
            for way in range(2):
                send_hidden(u, 1, way, 2)
        for way in range(2):
            send_hidden(u, 0, way, 1)

    def op_a(u, s, way):
        if GATHERS[u] == "two":
            arrived("a", u, 1, way)
            send_hidden(u, 2, way, 1)
            send_hidden(u, 3, way, 2)
        else:
            arrived("a", u, s - 1, way)
            send_hidden(u, s, way, 1)

    def op_pj(u):
        for way in range(2):
            if GATHERS[u] == "two":
                arrived("a", u, 0, way)
                arrived("a", u, 2, way)
            arrived("a", u, 3, way)
        load(2)

        @pl.loop(0, 2)
        def _(i):
            cols = pl.ds(pl.multiple_of(i * (width // 2), width // 2), width // 2)
            proj[u, :, cols] = jnp.dot(hid[u], wdn[:, cols], preferred_element_type=F32)

        send(("k", u), proj.at[u, plane(1 - k)], swap_in.at[u], k_s.at[u], k_r.at[u], sibling)

    def op_sc(u):
        arrived("k", u)
        for step in (2, 1, 3):
            there = lax.rem(x + step, 4)
            near = pl.ds(pl.multiple_of(there * ROWS, ROWS), ROWS)
            x_out[u, step - 1] = (proj[u, block(k, there), :] + swap_in[u, near, :]).astype(BF)
            send(("x", u, step), x_out.at[u, step - 1], x_in.at[u, step - 1], x_s.at[u, step - 1],
                 x_r.at[u, step - 1], at_x(step))

    def op_ty(u):
        shift, half = UNITS[u]
        near = pl.ds(pl.multiple_of(x * ROWS, ROWS), ROWS)
        total = proj[u, block(k, x), :] + swap_in[u, near, :]
        for step in (1, 3, 2):
            arrived("x", u, step)
            total += x_in[u, step - 1].astype(F32)
        if shift == 0:
            acc[pl.ds(half * ROWS, ROWS), :] = total
        else:
            y_out[shift - 1, half] = total
            send(("y", u), y_out.at[shift - 1, half], y_in.at[shift - 1, half], y_s.at[shift - 1, half],
                 y_r.at[shift - 1, half], at_y(shift))

    steps = {"x": op_x, "bx": op_bx, "by": op_by, "mm": op_mm, "r": op_r, "g": op_g, "a": op_a, "pj": op_pj,
             "sc": op_sc, "ty": op_ty}
    for step in ORDER:
        steps[step[0]](*step[1:])

    limit = jnp.where(c >= 4, lens[0, 1], lens[0, 0])
    for half in range(2):
        offset = lax.rem(c, 4) * (2 * ROWS) + half * ROWS + lax.broadcasted_iota(jnp.int32, (ROWS, 1), 0)
        keep = (offset < limit).astype(F32)
        total = acc[pl.ds(half * ROWS, ROWS), :]
        for shift in (1, 2, 3):
            arrived("y", SLOT[(shift, half)])
            total += y_in[shift - 1, half]
        out[pl.ds(half * ROWS, ROWS), :] = (total * keep).astype(BF)
    for copy in sent:
        copy.wait_send()


def local(activations, w_gate, w_up, w_down, seq_lengths):
    rows, depth = activations.shape
    ff = w_gate.shape[1]
    width = w_down.shape[1]
    dma = pltpu.SemaphoreType.DMA
    vmem = pl.BlockSpec(memory_space=pltpu.VMEM)
    hbm = pl.BlockSpec(memory_space=pl.ANY)
    return pl.pallas_call(
        kernel,
        out_shape=jax.ShapeDtypeStruct((rows, width), BF),
        in_specs=[vmem, hbm, hbm, hbm, pl.BlockSpec(memory_space=pltpu.SMEM)],
        out_specs=vmem,
        scratch_shapes=[
            pltpu.VMEM((N, UNIT, depth), BF),
            pltpu.VMEM((depth, 2 * ff), BF),
            pltpu.VMEM((ff, width), BF),
            pltpu.VMEM((N, UNIT, 2 * ff), F32),
            pltpu.VMEM((N, 2, 4, ROWS, 2 * ff), BF),
            pltpu.VMEM((N, 2, 4, ROWS, 2 * ff), BF),
            pltpu.VMEM((N_WIDE, 2, ROWS, 2 * ff), F32),
            pltpu.VMEM((N_WIDE, 2, ROWS, 2 * ff), F32),
            pltpu.VMEM((N, UNIT, ff), BF),
            pltpu.VMEM((N, UNIT, width), F32),
            pltpu.VMEM((N, UNIT // 2, width), F32),
            pltpu.VMEM((N, 3, ROWS, width), BF),
            pltpu.VMEM((N, 3, ROWS, width), BF),
            pltpu.VMEM((3, 2, ROWS, width), F32),
            pltpu.VMEM((3, 2, ROWS, width), F32),
            pltpu.VMEM((rows, width), F32),
            dma((3,)),
            dma((2, 3)), dma((2, 3)),
            dma((N, 4)), dma((N, 4)),
            dma((N, 4)), dma((N, 4)),
            dma((N, 2, 4)), dma((N, 2, 4)),
            dma((N, 2, 4)), dma((N, 2, 4)),
            dma((N,)), dma((N,)),
            dma((N, 3)), dma((N, 3)),
            dma((3, 2)), dma((3, 2)),
        ],
        compiler_params=pltpu.CompilerParams(collective_id=0, has_side_effects=True, vmem_limit_bytes=60 * 2**20),
        cost_estimate=pl.CostEstimate(flops=6 * 1024 * depth * ff, bytes_accessed=6 * depth * ff,
                                      transcendentals=128 * ff),
    )(activations, w_gate, w_up, w_down, seq_lengths)


def solution(mesh):
    return jax.shard_map(
        local,
        mesh=mesh,
        in_specs=(
            P(("dp", "col"), "row"),
            P("row", ("dp", "col")),
            P("row", ("dp", "col")),
            P(("dp", "col"), "row"),
            P("dp", None),
        ),
        out_specs=P(("dp", "col"), "row"),
        check_vma=False,
    )
```

time: 366 us -> 102 us (0.28)
  waiting for transfers between devices: 322 us -> 0 us
  Pallas kernels: 0 us -> 99.2 us
  matrix products: 23.3 us -> 0 us
  between operations: 13.2 us -> 0.01 us
  other arithmetic: 5.46 us -> 0 us
    psum x1 -> x0, waiting for transfers between devices: 168 us -> none  [local(): summed = lax.psum(partial_value, 'row')]
    pallas_call x0 -> x1, Pallas kernels: none -> 99.2 us  [local(): pl.pallas_call(kernel, out_shape=jax.ShapeDtypeStruct((rows, width), BF),...]
    reduce_scatter x1 -> x0, waiting for transfers between devices: 96.7 us -> none  [local(): lax.psum_scatter(jnp.dot(hidden, w_down, preferred_element_type=jnp.float...]
    all_gather x1 -> x0, waiting for transfers between devices: 56.7 us -> none  [local(): panel = lax.all_gather(activations, ('dp', 'col'), axis=0, tiled=True)]
    dot_general x3 -> x0, matrix products: 23.3 us -> none  [the longest x1 12 us: local(): jnp.dot(hidden, w_down, preferred_element_type=jnp.float32)]
    concatenate x1 -> x0, other arithmetic: 3.66 us -> none  [local(): partial_value = jnp.concatenate([gate_part, up_part], axis=1)]
  transfers between devices with their start and end apart: 3 -> 0, of which waited for: 3 -> 0; matrix products, arithmetic and copies ran while one was open for 0% -> 0% of each run, Pallas kernels for 0% -> 0%
where the time goes in v1:
time: 102 us; the launch traced here: 101 us
  Pallas kernels  99.2 us (97%)
  local copies, waits for them, and re-layouts  1.57 us (2%)
    pallas_call x1, Pallas kernels, local(): pl.pallas_call(kernel, out_shape=jax.ShapeDtypeStruct((rows, width), BF),...  99.2 us

profile of v1, /device:TPU:9, one launch (start us, length us, event | category | flops | bytes accessed | tf_op | source)
XLA Modules:
  0.0 100.8 jit_solution(2685710785001700581)
XLA Ops:
  0.0 99.2 %shard_map.55 = bf16[32,2048]{1,0:T(8,128)(2,1)} custom-call(bf16[32,2048]{1,0:T(8,128)(2,1)} %act.1, bf16[2048,896]{1,0:T(8,128)(2,1)} %w_gate.1, bf16[2048,896]{1,0:T(8,128)(2,1)} %w_up.1, bf16[896,2048]{1,0:T(8,128)(2,1)} %w_down.1, s32[1,2]{1,0:T(1,128)} %lens.1), custom_call_target="tpu_custom_call" | custom-call | flops 11274289152 | bytes 11010048 | tf_op jit(solution)/shard_map/pallas_call | solution.py:283
  99.2 1.6 %copy.7 = bf16[32,2048]{1,0:T(8,128)(2,1)} copy(bf16[32,2048]{1,0:T(8,128)(2,1)} %shard_map.55) | data formatting | bytes 262144

commit v2 on v1

--- a/solution.py
+++ b/solution.py
@@ -9,42 +9,45 @@
 BF, F32 = jnp.bfloat16, jnp.float32
 ROWS = 16
 UNIT = 128
-UNITS = [(0, 0), (1, 0), (3, 0), (2, 0), (1, 1), (2, 1), (3, 1), (0, 1)]
-SUMS = ['two', 'chain', 'chain', 'chainf', 'chain', 'chain', 'chain', 'chain']
-GATHERS = ['chain', 'chain', 'chain', 'chain', 'chain', 'chain', 'chain', 'chain']
+UNITS = [(0, 0), (3, 0), (2, 1), (1, 1), (1, 0), (0, 1), (3, 1), (2, 0)]
+SUMS = ['two', 'chain', 'chainh', 'chainh', 'chainh', 'chain', 'chain', 'chainh']
+GATHERS = ['chain', 'two', 'two', 'two', 'two', 'chain', 'chain', 'two']
+X_WIDE = [0, 4]
+SPLIT = [0, 1, 2, 3, 5, 6, 7]
 ORDER = [
-    ("x", 0), ("x", 1), ("bx", 0, 1), ("bx", 0, 3), ("bx", 0, 2), ("bx", 1, 1), ("bx", 1, 3), ("mm", 0, 0),
-    ("mm", 0, 1), ("bx", 1, 2), ("mm", 7, 0), ("by", 1, 0), ("by", 3, 0), ("mm", 7, 1), ("mm", 1, 0),
-    ("mm", 1, 1), ("r", 0, 1, 1), ("r", 0, 1, 0), ("mm", 2, 0), ("mm", 2, 1), ("r", 1, 1, 0), ("r", 1, 1, 1),
-    ("by", 1, 1), ("by", 3, 1), ("r", 7, 1, 0), ("r", 7, 1, 1), ("mm", 4, 0), ("r", 2, 1, 1), ("g", 0),
-    ("r", 2, 1, 0), ("by", 2, 0), ("r", 1, 2, 1), ("r", 1, 2, 0), ("mm", 4, 1), ("mm", 3, 0), ("r", 2, 2, 1),
-    ("a", 0, 1, 0), ("a", 0, 1, 1), ("r", 4, 1, 0), ("mm", 3, 1), ("r", 1, 3, 1), ("r", 2, 2, 0), ("r", 1, 3, 0),
-    ("r", 4, 1, 1), ("r", 3, 1, 0), ("by", 2, 1), ("r", 2, 3, 1), ("a", 0, 2, 0), ("a", 0, 2, 1), ("mm", 6, 0),
-    ("mm", 5, 0), ("r", 2, 3, 0), ("r", 3, 1, 1), ("r", 4, 2, 0), ("mm", 5, 1), ("r", 4, 2, 1), ("g", 1),
-    ("mm", 6, 1), ("a", 0, 3, 0), ("r", 6, 1, 0), ("a", 0, 3, 1), ("r", 3, 2, 1), ("r", 5, 1, 0), ("r", 3, 2, 0),
-    ("r", 7, 2, 1), ("g", 2), ("r", 4, 3, 1), ("r", 5, 1, 1), ("a", 1, 1, 1), ("r", 4, 3, 0), ("r", 6, 1, 1),
-    ("a", 1, 1, 0), ("pj", 0), ("r", 3, 3, 1), ("r", 6, 2, 0), ("r", 7, 2, 0), ("r", 7, 3, 1), ("r", 5, 2, 0),
-    ("a", 2, 1, 1), ("sc", 0), ("r", 3, 3, 0), ("a", 2, 1, 0), ("r", 5, 2, 1), ("g", 4), ("a", 1, 2, 1),
-    ("a", 1, 2, 0), ("r", 6, 2, 1), ("r", 6, 3, 0), ("r", 7, 3, 0), ("ty", 0), ("r", 5, 3, 0), ("a", 2, 2, 1),
-    ("g", 3), ("r", 5, 3, 1), ("a", 2, 2, 0), ("a", 4, 1, 1), ("a", 4, 1, 0), ("a", 1, 3, 1), ("a", 1, 3, 0),
-    ("r", 6, 3, 1), ("a", 2, 3, 1), ("a", 3, 1, 1), ("g", 7), ("g", 5), ("a", 4, 2, 1), ("a", 3, 1, 0),
-    ("a", 2, 3, 0), ("a", 4, 2, 0), ("g", 6), ("pj", 1), ("a", 5, 1, 0), ("a", 7, 1, 1), ("a", 3, 2, 1),
-    ("a", 3, 2, 0), ("a", 5, 1, 1), ("pj", 2), ("a", 4, 3, 0), ("sc", 1), ("a", 4, 3, 1), ("a", 5, 2, 0),
-    ("a", 7, 2, 1), ("a", 6, 1, 1), ("a", 6, 1, 0), ("a", 3, 3, 0), ("a", 3, 3, 1), ("sc", 2), ("a", 5, 2, 1),
-    ("a", 7, 1, 0), ("pj", 4), ("a", 7, 3, 1), ("a", 5, 3, 0), ("a", 6, 2, 1), ("a", 6, 2, 0), ("pj", 3),
-    ("a", 5, 3, 1), ("a", 7, 2, 0), ("sc", 4), ("ty", 1), ("a", 6, 3, 1), ("a", 6, 3, 0), ("sc", 3), ("pj", 5),
-    ("a", 7, 3, 0), ("ty", 2), ("pj", 6), ("sc", 5), ("pj", 7), ("ty", 4), ("sc", 6), ("ty", 3), ("sc", 7),
-    ("ty", 5), ("ty", 6), ("ty", 7),
+    ("x", 0), ("x", 1), ("bx", 0, 1), ("bx", 0, 3), ("bx", 0, 2), ("bx", 1, 1), ("mm", 0, 0), ("mm", 0, 1),
+    ("bx", 1, 3), ("bx", 1, 2), ("mm", 5, 0), ("by", 1, 0), ("mm", 5, 1), ("by", 3, 0), ("mm", 4, 0),
+    ("mm", 4, 1), ("r", 0, 1, 1), ("r", 0, 1, 0), ("mm", 1, 0), ("mm", 1, 1), ("r", 5, 1, 0), ("by", 1, 1),
+    ("r", 5, 1, 1), ("by", 3, 1), ("r", 4, 1, 0), ("r", 4, 1, 1), ("mm", 3, 0), ("mm", 6, 0), ("mm", 3, 1),
+    ("g", 0), ("mm", 6, 1), ("r", 5, 2, 0), ("r", 1, 1, 0), ("r", 5, 2, 1), ("by", 2, 0), ("r", 1, 1, 1),
+    ("r", 4, 2, 0), ("r", 4, 2, 1), ("r", 3, 1, 0), ("mm", 7, 0), ("r", 6, 1, 0), ("r", 3, 1, 1), ("a", 0, 1, 0),
+    ("a", 0, 1, 1), ("mm", 7, 1), ("by", 2, 1), ("r", 6, 1, 1), ("r", 5, 3, 0), ("r", 5, 3, 1), ("r", 1, 2, 0),
+    ("mm", 2, 0), ("r", 1, 2, 1), ("mm", 2, 1), ("r", 4, 3, 1), ("r", 4, 3, 0), ("r", 3, 2, 0), ("r", 3, 2, 1),
+    ("r", 7, 1, 0), ("a", 0, 2, 1), ("r", 7, 1, 1), ("r", 6, 2, 0), ("a", 0, 2, 0), ("r", 6, 2, 1), ("g", 5),
+    ("r", 1, 3, 0), ("r", 1, 3, 1), ("r", 2, 1, 0), ("r", 2, 1, 1), ("g", 4), ("r", 3, 3, 0), ("r", 3, 3, 1),
+    ("a", 0, 3, 1), ("r", 7, 2, 0), ("r", 7, 2, 1), ("r", 6, 3, 0), ("a", 0, 3, 0), ("r", 6, 3, 1),
+    ("a", 5, 1, 0), ("a", 5, 1, 1), ("g", 1), ("r", 2, 2, 0), ("r", 2, 2, 1), ("a", 4, 2, 0), ("a", 4, 2, 1),
+    ("g", 3), ("r", 7, 3, 0), ("r", 7, 3, 1), ("pj", 0, 0), ("g", 6), ("pj", 0, 1), ("a", 5, 2, 0),
+    ("a", 5, 2, 1), ("sc", 0, 0), ("a", 1, 2, 0), ("a", 1, 2, 1), ("sc", 0, 1), ("r", 2, 3, 0), ("r", 2, 3, 1),
+    ("pj", 4), ("a", 3, 2, 0), ("a", 3, 2, 1), ("ty", 0, 0), ("sc", 4), ("g", 7), ("a", 6, 1, 0), ("a", 6, 1, 1),
+    ("a", 5, 3, 0), ("a", 5, 3, 1), ("ty", 0, 1), ("pj", 1, 0), ("pj", 1, 1), ("g", 2), ("sc", 1, 0),
+    ("sc", 1, 1), ("pj", 3, 0), ("pj", 3, 1), ("a", 7, 2, 0), ("a", 7, 2, 1), ("a", 6, 2, 0), ("sc", 3, 0),
+    ("a", 6, 2, 1), ("ty", 4), ("sc", 3, 1), ("pj", 5, 0), ("pj", 5, 1), ("a", 2, 2, 0), ("a", 2, 2, 1),
+    ("ty", 1, 0), ("sc", 5, 0), ("ty", 1, 1), ("sc", 5, 1), ("a", 6, 3, 0), ("pj", 7, 0), ("a", 6, 3, 1),
+    ("pj", 7, 1), ("ty", 3, 0), ("sc", 7, 0), ("ty", 3, 1), ("pj", 2, 0), ("sc", 7, 1), ("pj", 2, 1),
+    ("pj", 6, 0), ("sc", 2, 0), ("ty", 5, 0), ("pj", 6, 1), ("ty", 5, 1), ("sc", 2, 1), ("sc", 6, 0),
+    ("ty", 7, 0), ("sc", 6, 1), ("ty", 7, 1), ("ty", 2, 0), ("ty", 2, 1), ("ty", 6, 0), ("ty", 6, 1),
 ]
 SLOT = {unit: i for i, unit in enumerate(UNITS)}
 N = len(UNITS)
-WIDE = [u for u in range(N) if SUMS[u] == "chainf"]
+WIDE = [u for u in range(N) if SUMS[u] in ("chainf", "chainh")]
 N_WIDE = max(1, len(WIDE))
+N_X_WIDE = max(1, len(X_WIDE))
 
 
 def kernel(act, w_gate, w_up, w_down, lens, out, panel, wgu, wdn, part, rs_out, rs_in, wide_out, wide_in, hid, proj,
-           swap_in, x_out, x_in, y_out, y_in, acc, w_sem, ax_s, ax_r, ak_s, ak_r, ay_s, ay_r, rs_s, rs_r, ag_s, ag_r,
-           k_s, k_r, x_s, x_r, y_s, y_r):
+           swap_in, x_out, x_in, xw_out, xw_in, y_out, y_in, acc, w_sem, ax_s, ax_r, ak_s, ak_r, ay_s, ay_r, rs_s, rs_r, wd_s, wd_r, ag_s,
+           ag_r, k_s, k_r, x_s, x_r, y_s, y_r):
     y, z, c = lax.axis_index("dp"), lax.axis_index("row"), lax.axis_index("col")
     x, k = c // 2, lax.rem(c, 2)
     ff = w_gate.shape[1]
@@ -170,9 +173,13 @@
             send_sum(u, way, 2, every, 2)
         elif s == 3 and u in WIDE:
             i = WIDE.index(u)
-            wide_out[i, way] = part[u, rows, :] + rs_in[u, way, 2].astype(F32)
-            send(("r", u, s, way), wide_out.at[i, way], wide_in.at[i, way], rs_s.at[u, way, s], rs_r.at[u, way, s],
-                 at_z(sign[way]))
+            cols = every if SUMS[u] == "chainf" else got
+            wide_out[i, way, :, cols] = part[u, rows, cols] + rs_in[u, way, 2, :, cols].astype(F32)
+            send(("w", u, way), wide_out.at[i, way, :, cols], wide_in.at[i, way, :, cols], wd_s.at[i, way],
+                 wd_r.at[i, way], at_z(sign[way]))
+            if SUMS[u] == "chainh":
+                rs_out[u, way, s, :, rest] = (part[u, rows, rest] + rs_in[u, way, 2, :, rest].astype(F32)).astype(BF)
+                send_sum(u, way, s, rest, 1)
         else:
             if s == 1:
                 rs_out[u, way, s, :, got] = (part[u, rows, got] + rs_in[u, way, 0, :, got].astype(F32)).astype(BF)
@@ -191,17 +198,22 @@
 
     def op_g(u):
         rows = chunk(0)
-        total = part[u, rows, :]
+        gate, up = part[u, rows, first], part[u, rows, second]
         for way in range(2):
-            arrived("r", u, 3, way)
             if u in WIDE:
-                total += wide_in[WIDE.index(u), way]
-            else:
-                total += rs_in[u, way, 3].astype(F32)
+                arrived("w", u, way)
+            if SUMS[u] != "chainf":
+                arrived("r", u, 3, way)
             if SUMS[u] == "two":
                 arrived("r", u, 2, way)
-                total += rs_in[u, way, 2].astype(F32)
-        hid[u, rows, :] = (jax.nn.silu(total[:, :ff]) * total[:, ff:]).astype(BF)
+                gate += rs_in[u, way, 2, :, first].astype(F32)
+                up += rs_in[u, way, 2, :, second].astype(F32)
+            wide_gate = u in WIDE and (SUMS[u] == "chainf" or way == 0)
+            wide_up = u in WIDE and (SUMS[u] == "chainf" or way == 1)
+            i = WIDE.index(u) if u in WIDE else 0
+            gate += wide_in[i, way, :, first] if wide_gate else rs_in[u, way, 3, :, first].astype(F32)
+            up += wide_in[i, way, :, second] if wide_up else rs_in[u, way, 3, :, second].astype(F32)
+        hid[u, rows, :] = (jax.nn.silu(gate) * up).astype(BF)
         if GATHERS[u] == "two":
             for way in range(2):
                 send_hidden(u, 1, way, 2)
@@ -217,43 +229,62 @@
             arrived("a", u, s - 1, way)
             send_hidden(u, s, way, 1)
 
-    def op_pj(u):
-        for way in range(2):
-            if GATHERS[u] == "two":
-                arrived("a", u, 0, way)
-                arrived("a", u, 2, way)
-            arrived("a", u, 3, way)
+    def part_cols(i):
+        return slice(0, width) if i is None else slice(i * width // 2, (i + 1) * width // 2)
+
+    def op_pj(u, i=None):
+        if not i:
+            for way in range(2):
+                if GATHERS[u] == "two":
+                    arrived("a", u, 0, way)
+                    arrived("a", u, 2, way)
+                arrived("a", u, 3, way)
         load(2)
-
-        @pl.loop(0, 2)
-        def _(i):
-            cols = pl.ds(pl.multiple_of(i * (width // 2), width // 2), width // 2)
+        cols = part_cols(i)
+        if i is None:
+            @pl.loop(0, 2)
+            def _(n):
+                piece = pl.ds(pl.multiple_of(n * (width // 2), width // 2), width // 2)
+                proj[u, :, piece] = jnp.dot(hid[u], wdn[:, piece], preferred_element_type=F32)
+        else:
             proj[u, :, cols] = jnp.dot(hid[u], wdn[:, cols], preferred_element_type=F32)
-
-        send(("k", u), proj.at[u, plane(1 - k)], swap_in.at[u], k_s.at[u], k_r.at[u], sibling)
-
-    def op_sc(u):
-        arrived("k", u)
+        send(("k", u, i), proj.at[u, plane(1 - k), cols], swap_in.at[u, :, cols], k_s.at[u, i or 0],
+             k_r.at[u, i or 0], sibling)
+
+    def op_sc(u, i=None):
+        arrived("k", u, i)
+        cols = part_cols(i)
         for step in (2, 1, 3):
             there = lax.rem(x + step, 4)
             near = pl.ds(pl.multiple_of(there * ROWS, ROWS), ROWS)
-            x_out[u, step - 1] = (proj[u, block(k, there), :] + swap_in[u, near, :]).astype(BF)
-            send(("x", u, step), x_out.at[u, step - 1], x_in.at[u, step - 1], x_s.at[u, step - 1],
-                 x_r.at[u, step - 1], at_x(step))
-
-    def op_ty(u):
+            total = proj[u, block(k, there), cols] + swap_in[u, near, cols]
+            if u in X_WIDE:
+                w = X_WIDE.index(u)
+                source, target = xw_out.at[w, step - 1, :, cols], xw_in.at[w, step - 1, :, cols]
+                xw_out[w, step - 1, :, cols] = total
+            else:
+                source, target = x_out.at[u, step - 1, :, cols], x_in.at[u, step - 1, :, cols]
+                x_out[u, step - 1, :, cols] = total.astype(BF)
+            send(("x", u, step, i), source, target, x_s.at[u, step - 1, i or 0], x_r.at[u, step - 1, i or 0],
+                 at_x(step))
+
+    def op_ty(u, i=None):
         shift, half = UNITS[u]
+        cols = part_cols(i)
         near = pl.ds(pl.multiple_of(x * ROWS, ROWS), ROWS)
-        total = proj[u, block(k, x), :] + swap_in[u, near, :]
+        total = proj[u, block(k, x), cols] + swap_in[u, near, cols]
         for step in (1, 3, 2):
-            arrived("x", u, step)
-            total += x_in[u, step - 1].astype(F32)
+            arrived("x", u, step, i)
+            if u in X_WIDE:
+                total += xw_in[X_WIDE.index(u), step - 1, :, cols]
+            else:
+                total += x_in[u, step - 1, :, cols].astype(F32)
         if shift == 0:
-            acc[pl.ds(half * ROWS, ROWS), :] = total
+            acc[pl.ds(half * ROWS, ROWS), cols] = total
         else:
-            y_out[shift - 1, half] = total
-            send(("y", u), y_out.at[shift - 1, half], y_in.at[shift - 1, half], y_s.at[shift - 1, half],
-                 y_r.at[shift - 1, half], at_y(shift))
+            y_out[shift - 1, half, :, cols] = total
+            send(("y", u, i), y_out.at[shift - 1, half, :, cols], y_in.at[shift - 1, half, :, cols],
+                 y_s.at[shift - 1, half, i or 0], y_r.at[shift - 1, half, i or 0], at_y(shift))
 
     steps = {"x": op_x, "bx": op_bx, "by": op_by, "mm": op_mm, "r": op_r, "g": op_g, "a": op_a, "pj": op_pj,
              "sc": op_sc, "ty": op_ty}
@@ -266,7 +297,9 @@
         keep = (offset < limit).astype(F32)
         total = acc[pl.ds(half * ROWS, ROWS), :]
         for shift in (1, 2, 3):
-            arrived("y", SLOT[(shift, half)])
+            u = SLOT[(shift, half)]
+            for i in ((0, 1) if u in SPLIT else (None,)):
+                arrived("y", u, i)
             total += y_in[shift - 1, half]
         out[pl.ds(half * ROWS, ROWS), :] = (total * keep).astype(BF)
     for copy in sent:
@@ -299,6 +332,8 @@
             pltpu.VMEM((N, UNIT // 2, width), F32),
             pltpu.VMEM((N, 3, ROWS, width), BF),
             pltpu.VMEM((N, 3, ROWS, width), BF),
+            pltpu.VMEM((N_X_WIDE, 3, ROWS, width), F32),
+            pltpu.VMEM((N_X_WIDE, 3, ROWS, width), F32),
             pltpu.VMEM((3, 2, ROWS, width), F32),
             pltpu.VMEM((3, 2, ROWS, width), F32),
             pltpu.VMEM((rows, width), F32),
@@ -307,10 +342,11 @@
             dma((N, 4)), dma((N, 4)),
             dma((N, 4)), dma((N, 4)),
             dma((N, 2, 4)), dma((N, 2, 4)),
+            dma((N_WIDE, 2)), dma((N_WIDE, 2)),
             dma((N, 2, 4)), dma((N, 2, 4)),
-            dma((N,)), dma((N,)),
-            dma((N, 3)), dma((N, 3)),
-            dma((3, 2)), dma((3, 2)),
+            dma((N, 2)), dma((N, 2)),
+            dma((N, 3, 2)), dma((N, 3, 2)),
+            dma((3, 2, 2)), dma((3, 2, 2)),
         ],
         compiler_params=pltpu.CompilerParams(collective_id=0, has_side_effects=True, vmem_limit_bytes=60 * 2**20),
         cost_estimate=pl.CostEstimate(flops=6 * 1024 * depth * ff, bytes_accessed=6 * depth * ff,

time: 102 us -> 104 us (1.020); the launches traced: 101 us -> 104 us
  Pallas kernels: 99.2 us -> 103 us
    pallas_call x1, Pallas kernels: 99.2 us -> 103 us  [local(): pl.pallas_call(kernel, out_shape=jax.ShapeDtypeStruct((rows, width), BF),...]
where the time goes in v2:
time: 104 us
  Pallas kernels  103 us (99%)
  local copies, waits for them, and re-layouts  1.57 us (2%)
    pallas_call x1, Pallas kernels, local(): pl.pallas_call(kernel, out_shape=jax.ShapeDtypeStruct((rows, width), BF),...  103 us

profile of v2, /device:TPU:9, one launch (start us, length us, event | category | flops | bytes accessed | tf_op | source)
XLA Modules:
  0.0 104.3 jit_solution(9842450446309341814)
XLA Ops:
  0.0 102.7 %shard_map.55 = bf16[32,2048]{1,0:T(8,128)(2,1)} custom-call(bf16[32,2048]{1,0:T(8,128)(2,1)} %act.1, bf16[2048,896]{1,0:T(8,128)(2,1)} %w_gate.1, bf16[2048,896]{1,0:T(8,128)(2,1)} %w_up.1, bf16[896,2048]{1,0:T(8,128)(2,1)} %w_down.1, s32[1,2]{1,0:T(1,128)} %lens.1), custom_call_target="tpu_custom_call" | custom-call | flops 11274289152 | bytes 11010048 | tf_op jit(solution)/shard_map/pallas_call | solution.py:316
  102.7 1.6 %copy.7 = bf16[32,2048]{1,0:T(8,128)(2,1)} copy(bf16[32,2048]{1,0:T(8,128)(2,1)} %shard_map.55) | data formatting | bytes 262144

commit v3 on v2

--- a/solution.py
+++ b/solution.py
@@ -9,34 +9,34 @@
 BF, F32 = jnp.bfloat16, jnp.float32
 ROWS = 16
 UNIT = 128
-UNITS = [(0, 0), (3, 0), (2, 1), (1, 1), (1, 0), (0, 1), (3, 1), (2, 0)]
-SUMS = ['two', 'chain', 'chainh', 'chainh', 'chainh', 'chain', 'chain', 'chainh']
-GATHERS = ['chain', 'two', 'two', 'two', 'two', 'chain', 'chain', 'two']
-X_WIDE = [0, 4]
-SPLIT = [0, 1, 2, 3, 5, 6, 7]
+UNITS = [(0, 0), (1, 0), (3, 0), (2, 0), (1, 1), (2, 1), (3, 1), (0, 1)]
+SUMS = ['two', 'chainh', 'chainh', 'chainh', 'chain', 'chain', 'chain', 'chain']
+GATHERS = ['chain', 'chain', 'chain', 'chain', 'chain', 'chain', 'chain', 'chain']
+X_WIDE = [0]
+SPLIT = []
 ORDER = [
-    ("x", 0), ("x", 1), ("bx", 0, 1), ("bx", 0, 3), ("bx", 0, 2), ("bx", 1, 1), ("mm", 0, 0), ("mm", 0, 1),
-    ("bx", 1, 3), ("bx", 1, 2), ("mm", 5, 0), ("by", 1, 0), ("mm", 5, 1), ("by", 3, 0), ("mm", 4, 0),
-    ("mm", 4, 1), ("r", 0, 1, 1), ("r", 0, 1, 0), ("mm", 1, 0), ("mm", 1, 1), ("r", 5, 1, 0), ("by", 1, 1),
-    ("r", 5, 1, 1), ("by", 3, 1), ("r", 4, 1, 0), ("r", 4, 1, 1), ("mm", 3, 0), ("mm", 6, 0), ("mm", 3, 1),
-    ("g", 0), ("mm", 6, 1), ("r", 5, 2, 0), ("r", 1, 1, 0), ("r", 5, 2, 1), ("by", 2, 0), ("r", 1, 1, 1),
-    ("r", 4, 2, 0), ("r", 4, 2, 1), ("r", 3, 1, 0), ("mm", 7, 0), ("r", 6, 1, 0), ("r", 3, 1, 1), ("a", 0, 1, 0),
-    ("a", 0, 1, 1), ("mm", 7, 1), ("by", 2, 1), ("r", 6, 1, 1), ("r", 5, 3, 0), ("r", 5, 3, 1), ("r", 1, 2, 0),
-    ("mm", 2, 0), ("r", 1, 2, 1), ("mm", 2, 1), ("r", 4, 3, 1), ("r", 4, 3, 0), ("r", 3, 2, 0), ("r", 3, 2, 1),
-    ("r", 7, 1, 0), ("a", 0, 2, 1), ("r", 7, 1, 1), ("r", 6, 2, 0), ("a", 0, 2, 0), ("r", 6, 2, 1), ("g", 5),
-    ("r", 1, 3, 0), ("r", 1, 3, 1), ("r", 2, 1, 0), ("r", 2, 1, 1), ("g", 4), ("r", 3, 3, 0), ("r", 3, 3, 1),
-    ("a", 0, 3, 1), ("r", 7, 2, 0), ("r", 7, 2, 1), ("r", 6, 3, 0), ("a", 0, 3, 0), ("r", 6, 3, 1),
-    ("a", 5, 1, 0), ("a", 5, 1, 1), ("g", 1), ("r", 2, 2, 0), ("r", 2, 2, 1), ("a", 4, 2, 0), ("a", 4, 2, 1),
-    ("g", 3), ("r", 7, 3, 0), ("r", 7, 3, 1), ("pj", 0, 0), ("g", 6), ("pj", 0, 1), ("a", 5, 2, 0),
-    ("a", 5, 2, 1), ("sc", 0, 0), ("a", 1, 2, 0), ("a", 1, 2, 1), ("sc", 0, 1), ("r", 2, 3, 0), ("r", 2, 3, 1),
-    ("pj", 4), ("a", 3, 2, 0), ("a", 3, 2, 1), ("ty", 0, 0), ("sc", 4), ("g", 7), ("a", 6, 1, 0), ("a", 6, 1, 1),
-    ("a", 5, 3, 0), ("a", 5, 3, 1), ("ty", 0, 1), ("pj", 1, 0), ("pj", 1, 1), ("g", 2), ("sc", 1, 0),
-    ("sc", 1, 1), ("pj", 3, 0), ("pj", 3, 1), ("a", 7, 2, 0), ("a", 7, 2, 1), ("a", 6, 2, 0), ("sc", 3, 0),
-    ("a", 6, 2, 1), ("ty", 4), ("sc", 3, 1), ("pj", 5, 0), ("pj", 5, 1), ("a", 2, 2, 0), ("a", 2, 2, 1),
-    ("ty", 1, 0), ("sc", 5, 0), ("ty", 1, 1), ("sc", 5, 1), ("a", 6, 3, 0), ("pj", 7, 0), ("a", 6, 3, 1),
-    ("pj", 7, 1), ("ty", 3, 0), ("sc", 7, 0), ("ty", 3, 1), ("pj", 2, 0), ("sc", 7, 1), ("pj", 2, 1),
-    ("pj", 6, 0), ("sc", 2, 0), ("ty", 5, 0), ("pj", 6, 1), ("ty", 5, 1), ("sc", 2, 1), ("sc", 6, 0),
-    ("ty", 7, 0), ("sc", 6, 1), ("ty", 7, 1), ("ty", 2, 0), ("ty", 2, 1), ("ty", 6, 0), ("ty", 6, 1),
+    ("x", 0), ("x", 1), ("bx", 0, 1), ("bx", 0, 3), ("bx", 0, 2), ("bx", 1, 1), ("bx", 1, 3), ("mm", 0, 0),
+    ("mm", 0, 1), ("bx", 1, 2), ("mm", 7, 0), ("by", 1, 0), ("by", 3, 0), ("mm", 7, 1), ("mm", 1, 0),
+    ("mm", 1, 1), ("r", 0, 1, 1), ("r", 0, 1, 0), ("mm", 2, 0), ("mm", 2, 1), ("r", 1, 1, 0), ("r", 1, 1, 1),
+    ("by", 1, 1), ("by", 3, 1), ("r", 7, 1, 0), ("r", 7, 1, 1), ("mm", 4, 0), ("r", 2, 1, 1), ("g", 0),
+    ("r", 2, 1, 0), ("by", 2, 0), ("r", 1, 2, 1), ("r", 1, 2, 0), ("mm", 4, 1), ("mm", 3, 0), ("r", 2, 2, 1),
+    ("a", 0, 1, 0), ("a", 0, 1, 1), ("r", 4, 1, 0), ("mm", 3, 1), ("r", 1, 3, 1), ("r", 2, 2, 0), ("r", 1, 3, 0),
+    ("r", 4, 1, 1), ("r", 3, 1, 0), ("by", 2, 1), ("r", 2, 3, 1), ("a", 0, 2, 0), ("a", 0, 2, 1), ("mm", 6, 0),
+    ("mm", 5, 0), ("r", 2, 3, 0), ("r", 3, 1, 1), ("r", 4, 2, 0), ("mm", 5, 1), ("r", 4, 2, 1), ("g", 1),
+    ("mm", 6, 1), ("a", 0, 3, 0), ("r", 6, 1, 0), ("a", 0, 3, 1), ("r", 3, 2, 1), ("r", 5, 1, 0), ("r", 3, 2, 0),
+    ("r", 7, 2, 1), ("g", 2), ("r", 4, 3, 1), ("r", 5, 1, 1), ("a", 1, 1, 1), ("r", 4, 3, 0), ("r", 6, 1, 1),
+    ("a", 1, 1, 0), ("pj", 0), ("r", 3, 3, 1), ("r", 6, 2, 0), ("r", 7, 2, 0), ("r", 7, 3, 1), ("r", 5, 2, 0),
+    ("a", 2, 1, 1), ("sc", 0), ("r", 3, 3, 0), ("a", 2, 1, 0), ("r", 5, 2, 1), ("g", 4), ("a", 1, 2, 1),
+    ("a", 1, 2, 0), ("r", 6, 2, 1), ("r", 6, 3, 0), ("r", 7, 3, 0), ("ty", 0), ("r", 5, 3, 0), ("a", 2, 2, 1),
+    ("g", 3), ("r", 5, 3, 1), ("a", 2, 2, 0), ("a", 4, 1, 1), ("a", 4, 1, 0), ("a", 1, 3, 1), ("a", 1, 3, 0),
+    ("r", 6, 3, 1), ("a", 2, 3, 1), ("a", 3, 1, 1), ("g", 7), ("g", 5), ("a", 4, 2, 1), ("a", 3, 1, 0),
+    ("a", 2, 3, 0), ("a", 4, 2, 0), ("g", 6), ("pj", 1), ("a", 5, 1, 0), ("a", 7, 1, 1), ("a", 3, 2, 1),
+    ("a", 3, 2, 0), ("a", 5, 1, 1), ("pj", 2), ("a", 4, 3, 0), ("sc", 1), ("a", 4, 3, 1), ("a", 5, 2, 0),
+    ("a", 7, 2, 1), ("a", 6, 1, 1), ("a", 6, 1, 0), ("a", 3, 3, 0), ("a", 3, 3, 1), ("sc", 2), ("a", 5, 2, 1),
+    ("a", 7, 1, 0), ("pj", 4), ("a", 7, 3, 1), ("a", 5, 3, 0), ("a", 6, 2, 1), ("a", 6, 2, 0), ("pj", 3),
+    ("a", 5, 3, 1), ("a", 7, 2, 0), ("sc", 4), ("ty", 1), ("a", 6, 3, 1), ("a", 6, 3, 0), ("sc", 3), ("pj", 5),
+    ("a", 7, 3, 0), ("ty", 2), ("pj", 6), ("sc", 5), ("pj", 7), ("ty", 4), ("sc", 6), ("ty", 3), ("sc", 7),
+    ("ty", 5), ("ty", 6), ("ty", 7),
 ]
 SLOT = {unit: i for i, unit in enumerate(UNITS)}
 N = len(UNITS)

time: 104 us -> 103 us (level)
  no operation moved by 1% of the time
where the time goes in v3:
time: 103 us
  Pallas kernels  102 us (99%)
  local copies, waits for them, and re-layouts  1.57 us (2%)
    pallas_call x1, Pallas kernels, local(): pl.pallas_call(kernel, out_shape=jax.ShapeDtypeStruct((rows, width), BF),...  102 us

profile of v3, /device:TPU:9, one launch (start us, length us, event | category | flops | bytes accessed | tf_op | source)
XLA Modules:
  0.0 103.3 jit_solution(9129831071326430190)
XLA Ops:
  0.0 101.7 %shard_map.55 = bf16[32,2048]{1,0:T(8,128)(2,1)} custom-call(bf16[32,2048]{1,0:T(8,128)(2,1)} %act.1, bf16[2048,896]{1,0:T(8,128)(2,1)} %w_gate.1, bf16[2048,896]{1,0:T(8,128)(2,1)} %w_up.1, bf16[896,2048]{1,0:T(8,128)(2,1)} %w_down.1, s32[1,2]{1,0:T(1,128)} %lens.1), custom_call_target="tpu_custom_call" | custom-call | flops 11274289152 | bytes 11010048 | tf_op jit(solution)/shard_map/pallas_call | solution.py:316
  101.7 1.6 %copy.7 = bf16[32,2048]{1,0:T(8,128)(2,1)} copy(bf16[32,2048]{1,0:T(8,128)(2,1)} %shard_map.55) | data formatting | bytes 262144
